TPU v7x, 32 devices: a whole 2x2x4 slice. The times are simulated.
32 devices in a mesh: dp: 4 (over z), pipe: 4 (over y, x), tensor: 2 (over core).
Axes of the slice: x: 2, y: 2, z: 4, core: 2. Of those that a mesh axis runs over, the one named last changes fastest.
Arguments:
- section_out: bfloat16 [4, 512, 12288], P('pipe', 'dp', 'tensor'), may hold values from -6 to 6
- embedded: bfloat16 [512, 12288], P('dp', 'tensor'), may hold values from -6 to 6
- cot_norm: bfloat16 [4, 512, 12288], P('pipe', 'dp', 'tensor'), may hold values from -3 to 3
- cot_res: bfloat16 [4, 512, 12288], P('pipe', 'dp', 'tensor'), may hold values from -3 to 3
- gain: bfloat16 [4, 64, 12288], P('pipe', None, 'tensor'), may hold values from 0.25 to 1.75
- bias: bfloat16 [4, 64, 12288], P('pipe', None, 'tensor'), may hold values from -1.5 to 1.5
- lang_ids: int32 [512], P('dp'), may hold values from 0 to 63
- mb_order: int32 [4, 4], P('dp'), may hold values from 0 to 3, each once within a row
Outputs:
- normed_out: bfloat16 [4, 512, 12288], P('pipe', 'dp', 'tensor')
- returned_grad: bfloat16 [4, 512, 12288], P('pipe', 'dp', 'tensor')
- gain_grad: float32 [4, 64, 12288], P('pipe', None, 'tensor')
- bias_grad: float32 [4, 64, 12288], P('pipe', None, 'tensor')
Inputs may be any that keep to these rules, and one draw needn't show every extreme that they name: `lang_ids`: a language id for every token. `mb_order`: each replica's row is a permutation of the 4 micro-batches.
All inputs are finite; a program needn't handle non-finite values.
Results may differ from a plain program's by a relative error of at most 0.0004.
Values may be sent and summed in bfloat16 or wider, within the bound.
A program may use at most 64 MiB of HBM per device.

v0:
```python
import jax
import jax.numpy as jnp
from jax import lax
from jax.sharding import PartitionSpec as P

D = 12288
MB = 4


eps = 1e-05


def shifted(value, axis, steps):
    count = lax.axis_size(axis)
    leading, last = (max(0, -steps), min(count, count - steps))
    return lax.ppermute(value, axis, [(source, source + steps) for source in range(leading, last)])


def passed_along(array, axis, by):
    length = lax.axis_size(axis)
    return lax.ppermute(array, axis, [(i, (i + by) % length) for i in range(length)])


def reorder(values, order):
    shaped = values.reshape((MB, -1) + values.shape[1:])
    return jnp.take(shaped, order, axis=0).reshape(values.shape)


def invert(order):
    slots = jnp.arange(MB, dtype=jnp.int32)
    hits = (order[:, None] == slots[None, :]).astype(jnp.int32)
    return jnp.sum(slots[:, None] * hits, axis=0)


def local(section_out, embedded, cot_norm, cot_res, gain, bias, lang_ids, mb_order):
    local_width = embedded.shape[1]
    langs = gain.shape[1]
    received = shifted(section_out, "pipe", 1)
    is_first = lax.axis_index("pipe") == 0
    inputs = jnp.where(is_first, embedded, received[0]).astype(jnp.float32)
    order = mb_order[0]
    inverse = invert(order)
    cot_fwd = reorder(cot_norm[0], inverse).astype(jnp.float32)
    pass_fwd = reorder(cot_res[0], inverse).astype(jnp.float32)
    matches = lang_ids[:, None] == jnp.arange(langs, dtype=jnp.int32)[None, :]
    selector = matches.astype(jnp.bfloat16)
    gain_rows = jnp.dot(selector, gain[0], preferred_element_type=jnp.float32)
    bias_rows = jnp.dot(selector, bias[0], preferred_element_type=jnp.float32)
    scaled_cot = cot_fwd * gain_rows
    moment_one, moment_two = lax.psum(
        (jnp.sum(inputs, axis=1), jnp.sum(inputs * inputs, axis=1)), "tensor"
    )
    center = moment_one[:, None] / D
    spread = moment_two[:, None] / D - center * center
    inv_scale = lax.rsqrt(spread + eps)
    normalized = (inputs - center) * inv_scale
    cot_total, cross_total = lax.psum(
        (jnp.sum(scaled_cot, axis=1), jnp.sum(scaled_cot * normalized, axis=1)), "tensor"
    )
    mean_cot = cot_total[:, None] / D
    mean_cross = cross_total[:, None] / D
    normed = (normalized * gain_rows + bias_rows).astype(jnp.bfloat16)
    input_grad = (pass_fwd + inv_scale * (scaled_cot - mean_cot - normalized * mean_cross)).astype(
        jnp.bfloat16
    )
    sent_back = reorder(input_grad, order)
    returned = passed_along(sent_back[None], "pipe", -1)
    products = jnp.concatenate([cot_fwd * normalized, cot_fwd], axis=1)
    local_sums = jnp.dot(
        matches.astype(jnp.float32).T,
        products,
        precision=lax.Precision.HIGHEST,
        preferred_element_type=jnp.float32,
    )
    summed = lax.psum(local_sums, "dp")
    return (normed[None], returned, summed[:, :local_width][None], summed[:, local_width:][None])


def solution(mesh):
    return jax.shard_map(
        local,
        mesh=mesh,
        in_specs=(
            P("pipe", "dp", "tensor"),
            P("dp", "tensor"),
            P("pipe", "dp", "tensor"),
            P("pipe", "dp", "tensor"),
            P("pipe", None, "tensor"),
            P("pipe", None, "tensor"),
            P("dp"),
            P("dp", None),
        ),
        out_specs=(
            P("pipe", "dp", "tensor"),
            P("pipe", "dp", "tensor"),
            P("pipe", None, "tensor"),
            P("pipe", None, "tensor"),
        ),
        check_vma=False,
    )
```

profile of v0, /device:TPU:0, one launch (start us, length us, event | category | flops | bytes accessed | tf_op | source)
XLA Modules:
  0.0 198.0 jit_solution(2647325105909903910)
XLA Ops:
  7.2 0.0 copy-start
  7.2 0.0 copy-start.4
  7.2 0.0 all-reduce.4.cloned.1.call-start
  7.2 6.3 %collective-permute-start = (bf16[1,128,6144]{2,1,0:T(8,128)(2,1)}, bf16[1,128,6144]{2,1,0:T(8,128)(2,1)}, u32[]{:S(2)}, u32[]{:S(2)}) collective-permute-start(bf16[1,128,6144]{2,1,0:T(8,128)(2,1)} %param.10), channel_id=1, source_target_pairs={{0,2},{2,4},{4,6},{1,3},{3,5},{5,7},{8,10},{10,12},{12,14},{9,11},... | collective-permute-start | bytes 4718600 | tf_op jit(solution)/shard_map/ppermute | solution.py:16
  13.5 0.7 select_reduce_fusion
  14.3 0.7 compare_select_fusion
  14.9 0.7 compare_and_fusion
  15.6 0.0 copy-done
  15.6 1.8 gather_fusion
  17.4 0.0 copy-done.4
  17.4 1.8 gather_fusion.1
  19.2 3.4 %broadcast_select_fusion.1 = (bf16[4,32,6144]{2,1,0:T(8,128)(2,1)S(1)}, bf16[4,32,6144]{2,1,0:T(8,128)(2,1)}) fusion(bf16[4,32,6144]{2,1,0:T(8,128)(2,1)} %gather_fusion.1, pred[4]{0:T(512)(128)(4,1)S(1)} %compare_and_fusion.1, bf16[4,32,6144]{2,1,0:T(8,128)(2,1)} %gather_fusion), kind=kLoop, calls=%fused_computation.30 | loop fusion | flops 1572864 | bytes 6291460 | tf_op jit(solution)/shard_map/jit(_take)/select_n | solution.py:26
  22.5 0.0 copy-start.5
  22.6 2.1 %bitcast_convert_fusion = f32[128,6144]{1,0:T(8,128)} fusion(bf16[4,32,6144]{2,1,0:T(8,128)(2,1)S(1)} %get-tuple-element.17), kind=kLoop, calls=%fused_computation.27 | loop fusion | flops 786432 | bytes 4718592 | tf_op jit(solution)/shard_map/convert_element_type | solution.py:43
  24.7 0.0 copy-start.6
  24.7 21.6 %collective-permute-done = bf16[1,128,6144]{2,1,0:T(8,128)(2,1)} collective-permute-done((bf16[1,128,6144]{2,1,0:T(8,128)(2,1)}, bf16[1,128,6144]{2,1,0:T(8,128)(2,1)}, u32[]{:S(2)}, u32[]{:S(2)}) %collective-permute-start) | collective-permute-done | bytes 1572896 | tf_op jit(solution)/shard_map/ppermute | solution.py:16
  46.3 0.0 copy-done.5
  46.3 3.4 %convert_reduce_fusion = (f32[128]{0:T(128)S(1)}, f32[128]{0:T(128)S(1)}, bf16[128,6144]{1,0:T(8,128)(2,1)}) fusion(bf16[128,6144]{1,0:T(8,128)(2,1)S(1)} %copy-done.5, bf16[1,128,6144]{2,1,0:T(8,128)(2,1)} %collective-permute-done, pred[]{:T(512)S(6)} %eq.31), kind=kLoop, calls=%fused_computation.12 | loop fusion | flops 3931904 | bytes 4719617 | tf_op jit(solution)/shard_map/reduce_sum | solution.py:51
  49.7 2.4 %all-reduce.1 = (f32[128]{0:T(128)S(1)}, f32[128]{0:T(128)S(1)}) all-reduce(f32[128]{0:T(128)S(1)} %get-tuple-element.8, f32[128]{0:T(128)S(1)} %get-tuple-element.7), channel_id=1, replica_groups=mesh['dp'=4,'pipe'=4,'tensor'=2] {'tensor'}, use_global_device_ids=true, to_apply=%region_3.4 | all-reduce | flops 256 | bytes 2048 | tf_op jit(solution)/shard_map/psum | solution.py:50
  52.1 0.0 copy-done.6
  52.1 0.0 copy-start.3
  52.1 4.6 %fusion.17 = (f32[128]{0:T(128)S(1)}, f32[128]{0:T(128)S(1)}, f32[128,6144]{1,0:T(8,128)S(1)}, f32[128,6144]{1,0:T(8,128)}) fusion(bf16[4,32,6144]{2,1,0:T(8,128)(2,1)S(1)} %get-tuple-element.17, f32[128]{0:T(128)S(1)} %get-tuple-element.20, f32[128]{0:T(128)S(1)} %get-tuple-element.19, bf16[128,6144]{1,0:T(8,128)(2,1)} %get-tuple-element.13, ...), kind=kOutput, calls=%fused_computation.32 | convolution fusion | flops 107749120 | bytes 10226176 | tf_op jit(solution)/shard_map/dot_general | solution.py:47
  56.8 0.0 copy-done.3
  56.8 4.4 %fusion.2 = f32[64,12288]{1,0:T(8,128)} fusion(f32[128,6144]{1,0:T(8,128)S(1)} %copy-done.3, f32[128,6144]{1,0:T(8,128)S(1)} %get-tuple-element.14, s32[128]{0:T(128)S(1)} %copy-done.6), kind=kOutput, calls=%fused_computation.6 | convolution fusion | flops 1209540608 | bytes 9437696 | tf_op jit(solution)/shard_map/dot_general | solution.py:69
  61.1 0.0 all-reduce.4.cloned.1.call-update
  61.2 2.5 %all-reduce = (f32[128]{0:T(128)S(1)}, f32[128]{0:T(128)S(1)}) all-reduce(f32[128]{0:T(128)S(1)} %get-tuple-element.6, f32[128]{0:T(128)S(1)} %get-tuple-element.5), channel_id=1, replica_groups=mesh['dp'=4,'pipe'=4,'tensor'=2] {'tensor'}, use_global_device_ids=true, to_apply=%region_8.10 | all-reduce | flops 256 | bytes 2048 | tf_op jit(solution)/shard_map/psum | solution.py:57
  63.7 5.6 %fusion.15 = bf16[128,6144]{1,0:T(8,128)(2,1)} fusion(bf16[128,6144]{1,0:T(8,128)(2,1)} %get-tuple-element.13, bf16[4,32,6144]{2,1,0:T(8,128)(2,1)} %get-tuple-element.18, f32[128]{0:T(128)S(1)} %get-tuple-element.22, f32[128]{0:T(128)S(1)} %get-tuple-element.23, f32[128]{0:T(128)S(1)} %get-tuple-element.20, f32[128]{0:T(128)S(1)} %get-tuple-element.19, ...), kind=kLoop, calls=%fused_computation.22 | loop fusion | flops 9437184 | bytes 9439232 | tf_op jit(solution)/shard_map/convert_element_type | solution.py:63
  69.2 0.0 copy-start.2
  69.2 3.3 %gather_fusion.2 = bf16[4,32,6144]{2,1,0:T(8,128)(2,1)} fusion(bf16[4,32,6144]{2,1,0:T(8,128)(2,1)} %bitcast.40, s32[1024]{0:T(1024)S(1)} %pad_clamp_fusion), kind=kCustom, calls=%fused_computation.2.clone | custom fusion | bytes 3145744 | tf_op jit(solution)/shard_map/jit(_take)/gather | solution.py:26
  72.6 0.0 copy-start.1
  72.6 1.8 broadcast_select_fusion
  74.3 3.5 %collective-permute-start.1 = (bf16[1,128,6144]{2,1,0:T(8,128)(2,1)S(1)}, bf16[1,128,6144]{2,1,0:T(8,128)(2,1)}, u32[]{:S(2)}, u32[]{:S(2)}) collective-permute-start(bf16[1,128,6144]{2,1,0:T(8,128)(2,1)S(1)} %bitcast.42), channel_id=1, source_target_pairs={{0,6},{2,0},{4,2},{6,4},{1,7},{3,1},{5,3},{7,5},{8,14},{10,8},{12,... | collective-permute-start | bytes 4718600 | tf_op jit(solution)/shard_map/ppermute | solution.py:21
  77.8 0.0 copy-done.2
  77.8 0.0 copy-done.1
  77.8 3.1 %fusion.1 = bf16[1,128,6144]{2,1,0:T(8,128)(2,1)} fusion(f32[128,6144]{1,0:T(8,128)S(1)} %copy-done.1, bf16[128,6144]{1,0:T(8,128)(2,1)S(1)} %copy-done.2, f32[128]{0:T(128)S(1)} %get-tuple-element.20, f32[128]{0:T(128)S(1)} %get-tuple-element.19, bf16[1,64,6144]{2,1,0:T(8,128)(2,1)} %param.15, s32[128]{0:T(128)S(1)} %copy-done.6), kind=kOutput, calls=%fused_computation.5 | convolution fusion | flops 105390080 | bytes 7079424 | tf_op jit(solution)/shard_map/dot_general | solution.py:48
  80.9 30.8 %collective-permute-done.1 = bf16[1,128,6144]{2,1,0:T(8,128)(2,1)} collective-permute-done((bf16[1,128,6144]{2,1,0:T(8,128)(2,1)S(1)}, bf16[1,128,6144]{2,1,0:T(8,128)(2,1)}, u32[]{:S(2)}, u32[]{:S(2)}) %collective-permute-start.1) | collective-permute-done | bytes 1572896 | tf_op jit(solution)/shard_map/ppermute | solution.py:21
  111.8 72.8 %all-reduce.4.cloned.1.call-done = f32[64,12288]{1,0:T(8,128)} async-done(((f32[64,12288]{1,0:T(8,128)}), f32[64,12288]{1,0:T(8,128)}) %all-reduce.4.cloned.1.call-update) | async-done | bytes 3145744 | tf_op jit(solution)/shard_map/psum | solution.py:75
  184.6 3.8 %slice_bitcast_fusion = (f32[1,64,6144]{2,1,0:T(8,128)}, f32[1,64,6144]{2,1,0:T(8,128)}) fusion(f32[64,12288]{1,0:T(8,128)} %all-reduce.4.cloned.1.call-done), kind=kLoop, calls=%fused_computation.24 | loop fusion | bytes 6291456 | tf_op jit(solution)/shard_map/broadcast_in_dim | solution.py:76
  188.5 2.7 %copy.14 = bf16[1,128,6144]{2,1,0:T(8,128)(2,1)} copy(bf16[1,128,6144]{2,1,0:T(8,128)(2,1)} %collective-permute-done.1) | data formatting | bytes 3145728
  (6 shorter events, 0.0 us)
Async XLA Ops:
  7.2 8.4 %copy-start = (bf16[1,128,6144]{2,1,0:T(8,128)(2,1)S(1)}, bf16[1,128,6144]{2,1,0:T(8,128)(2,1)}, u32[]{:S(2)}) copy-start(bf16[1,128,6144]{2,1,0:T(8,128)(2,1)} %param.13) | copy-start | bytes 4718596
  7.2 10.2 %copy-start.4 = (bf16[1,128,6144]{2,1,0:T(8,128)(2,1)S(1)}, bf16[1,128,6144]{2,1,0:T(8,128)(2,1)}, u32[]{:S(2)}) copy-start(bf16[1,128,6144]{2,1,0:T(8,128)(2,1)} %param.12) | copy-start | bytes 4718596
  7.2 177.5 %all-reduce.4.cloned.1.call-start = ((), (), s32[]{:S(2)}) async-start(), calls=%async_computation | async-start | bytes 6291456 | tf_op jit(solution)/shard_map/psum | solution.py:75
  7.2 39.1 %collective-permute-start = (bf16[1,128,6144]{2,1,0:T(8,128)(2,1)}, bf16[1,128,6144]{2,1,0:T(8,128)(2,1)}, u32[]{:S(2)}, u32[]{:S(2)}) collective-permute-start(bf16[1,128,6144]{2,1,0:T(8,128)(2,1)} %param.10), channel_id=1, source_target_pairs={{0,2},{2,4},{4,6},{1,3},{3,5},{5,7},{8,10},{10,12},{12,14},{9,11},... | collective-permute-start | bytes 4718600 | tf_op jit(solution)/shard_map/ppermute | solution.py:16
  22.5 23.8 %copy-start.5 = (bf16[128,6144]{1,0:T(8,128)(2,1)S(1)}, bf16[128,6144]{1,0:T(8,128)(2,1)}, u32[]{:S(2)}) copy-start(bf16[128,6144]{1,0:T(8,128)(2,1)} %param.11) | copy-start | bytes 4718596
  24.7 27.4 %copy-start.6 = (s32[128]{0:T(128)S(1)}, s32[128]{0:T(128)}, u32[]{:S(2)}) copy-start(s32[128]{0:T(128)} %param.16) | copy-start | bytes 1540
  52.1 4.6 %copy-start.3 = (f32[128,6144]{1,0:T(8,128)S(1)}, f32[128,6144]{1,0:T(8,128)}, u32[]{:S(2)}) copy-start(f32[128,6144]{1,0:T(8,128)} %bitcast_convert_fusion) | copy-start | bytes 9437188
  69.2 8.6 %copy-start.2 = (bf16[128,6144]{1,0:T(8,128)(2,1)S(1)}, bf16[128,6144]{1,0:T(8,128)(2,1)}, u32[]{:S(2)}) copy-start(bf16[128,6144]{1,0:T(8,128)(2,1)} %get-tuple-element.13) | copy-start | bytes 4718596
  72.6 5.2 %copy-start.1 = (f32[128,6144]{1,0:T(8,128)S(1)}, f32[128,6144]{1,0:T(8,128)}, u32[]{:S(2)}) copy-start(f32[128,6144]{1,0:T(8,128)} %get-tuple-element.21) | copy-start | bytes 9437188
  74.3 37.4 %collective-permute-start.1 = (bf16[1,128,6144]{2,1,0:T(8,128)(2,1)S(1)}, bf16[1,128,6144]{2,1,0:T(8,128)(2,1)}, u32[]{:S(2)}, u32[]{:S(2)}) collective-permute-start(bf16[1,128,6144]{2,1,0:T(8,128)(2,1)S(1)} %bitcast.42), channel_id=1, source_target_pairs={{0,6},{2,0},{4,2},{6,4},{1,7},{3,1},{5,3},{7,5},{8,14},{10,8},{12,... | collective-permute-start | bytes 4718600 | tf_op jit(solution)/shard_map/ppermute | solution.py:21
Sparse Core Ops, SparseCore 0:
  61.3 123.3 all-reduce.3
where the time goes:
time: 198 us
  waiting for transfers between devices  125 us (63%)
  other arithmetic  18.3 us (9%)
  between operations  14.1 us (7%)
  local copies, waits for them, and re-layouts  13.5 us (7%)
  matrix products  12.1 us (6%)
  starting transfers between devices  9.77 us (5%)
  blocking collectives  4.91 us (2%)
    psum x1, waiting for transfers between devices, local(): summed = lax.psum(local_sums, 'dp')  72.8 us
    ppermute x1, waiting for transfers between devices, passed_along(): lax.ppermute(array, axis, [(i, (i + by) % length) for i in range(length)])  30.8 us
    ppermute x1, waiting for transfers between devices, shifted(): lax.ppermute(value, axis, [(source, source + steps) for source in range(l...  21.6 us
    gather x3, local copies, waits for them, and re-layouts, reorder(): return jnp.take(shaped, order, axis=0).reshape(values.shape)  6.92 us
    ppermute x1, starting transfers between devices, shifted(): lax.ppermute(value, axis, [(source, source + steps) for source in range(l...  6.27 us
    select_n x4, other arithmetic, reorder(): return jnp.take(shaped, order, axis=0).reshape(values.shape)  5.8 us
    convert_element_type x1, other arithmetic, local(): (pass_fwd + inv_scale * (scaled_cot - mean_cot - normalized * mean_cross)...  5.57 us
    dot_general x1, matrix products, local(): gain_rows = jnp.dot(selector, gain[0], preferred_element_type=jnp.float32)  4.63 us
  transfers between devices with their start and end apart: 3, of which 3 were waited for; matrix products, arithmetic and copies ran while one was open for 13% of the time, Pallas kernels for 0%

commit v1 on v0

v1 whole, which is shorter than its diff:
```python
import functools

import jax
import jax.numpy as jnp
from jax import lax
from jax.experimental import pallas as pl
from jax.experimental.pallas import tpu as pltpu
from jax.sharding import PartitionSpec as P

D = 12288
MB = 4
EPS = 1e-05
CW = 384
AHEAD = 4
LANES = 128
MESH = pl.DeviceIdType.MESH
ANY = pl.BlockSpec(memory_space=pl.ANY)
VMEM = pl.BlockSpec(memory_space=pltpu.VMEM)
SMEM = pl.BlockSpec(memory_space=pltpu.SMEM)
F32 = jnp.float32
BF16 = jnp.bfloat16


def fold(value):
    total = value[:, :LANES]
    for start in range(LANES, value.shape[1], LANES):
        total = total + value[:, start : start + LANES]
    return total


def pack(first, second):
    lane = lax.broadcasted_iota(jnp.int32, first.shape, 1)
    one = jnp.sum(first, axis=1, keepdims=True)
    two = jnp.sum(second, axis=1, keepdims=True)
    return jnp.where(lane == 0, one, jnp.where(lane == 1, two, 0.0))


def kernel(
    n_dp, n_pipe, n_tensor,
    section, embedded, cot, res, gain, bias, lang, order,
    normed_out, grad_out, gain_out, bias_out,
    source, cot_raw, res_raw, x_buf, cot_fwd, xn_buf, sc_buf, n_buf, g_buf, g_tmp,
    own, came, tot, mom_own, mom_in, cross_own, cross_in, rows, sel_t2, sel,
    load_sem, x_send, x_recv, mom_send, mom_recv, cross_send, cross_recv,
    up_send, in_recv, tot_send, tot_recv, sum_out, n_out, g_send, g_recv,
):
    dp, pipe, tensor = lax.axis_index("dp"), lax.axis_index("pipe"), lax.axis_index("tensor")
    tokens, width = section.shape[1], section.shape[2]
    langs = gain.shape[0]
    per = tokens // MB
    count = width // CW
    half = n_dp // 2
    left = dp < half
    up = jnp.where(left, dp + 1, dp - 1)
    out = jnp.where(left, dp - 1, dp + 1)
    center = jnp.logical_or(dp == half - 1, dp == half)
    edge = jnp.logical_not(center)
    relay = jnp.logical_and(dp > 0, dp < n_dp - 1)
    after, before = lax.rem(pipe + 1, n_pipe), lax.rem(pipe + n_pipe - 1, n_pipe)
    first, last = pipe == 0, pipe == n_pipe - 1

    def columns(c):
        return pl.ds(pl.multiple_of(c * CW, CW), CW)

    @pl.when(last)
    def _():
        pltpu.make_async_copy(embedded, source, load_sem.at[0]).start()

    @pl.when(jnp.logical_not(last))
    def _():
        pltpu.make_async_copy(section.at[0], source, load_sem.at[0]).start()

    load_cot = pltpu.make_async_copy(cot, cot_raw, load_sem.at[1])
    load_res = pltpu.make_async_copy(res, res_raw, load_sem.at[2])
    load_cot.start()
    load_res.start()

    barrier = pltpu.get_barrier_semaphore()
    partners = 0
    for step in (1, n_dp - 1):
        pl.semaphore_signal(barrier, inc=1, device_id={"dp": lax.rem(dp + step, n_dp)}, device_id_type=MESH)
        partners += 1
    for t in range(n_tensor):
        other = lax.rem(tensor + t, n_tensor)
        for p in (after, before):
            pl.semaphore_signal(barrier, inc=1, device_id={"pipe": p, "tensor": other}, device_id_type=MESH)
            partners += 1
        if t:
            pl.semaphore_signal(barrier, inc=1, device_id={"tensor": other}, device_id_type=MESH)
            partners += 1

    picks = (lax.broadcasted_iota(jnp.int32, (langs, tokens), 0) == lang[...]).astype(F32)
    sel_t2[:, :tokens] = picks.astype(BF16)
    sel_t2[:, tokens:] = picks.astype(BF16)
    sel[...] = picks.T.astype(BF16)

    pltpu.make_async_copy(embedded, source, load_sem.at[0]).wait()
    zeros = jnp.zeros((tokens, LANES), F32)

    def moments(c, carry):
        x = source[:, columns(c)].astype(F32)
        return carry[0] + fold(x), carry[1] + fold(x * x)

    one, two = lax.fori_loop(0, count, moments, (zeros, zeros))
    mom_own[...] = pack(one, two)

    pl.semaphore_wait(barrier, partners)

    def send_moments(t):
        return pltpu.make_async_remote_copy(
            src_ref=mom_own, dst_ref=mom_in.at[tensor],
            send_sem=mom_send.at[t], recv_sem=mom_recv.at[tensor],
            device_id={"pipe": after, "tensor": lax.rem(tensor + t, n_tensor)}, device_id_type=MESH,
        )

    for t in range(n_tensor):
        send_moments(t).start()

    def send_x(c):
        return pltpu.make_async_remote_copy(
            src_ref=section.at[0, :, columns(c)], dst_ref=x_buf.at[c],
            send_sem=x_send.at[c], recv_sem=x_recv.at[c],
            device_id={"pipe": after}, device_id_type=MESH,
        )

    def load_x(c):
        return pltpu.make_async_copy(embedded.at[:, columns(c)], x_buf.at[c], x_recv.at[c])

    @pl.when(jnp.logical_not(last))
    def _():
        for c in range(min(AHEAD, count)):
            send_x(c).start()

    @pl.when(first)
    def _():
        @pl.loop(0, count)
        def _(c):
            load_x(c).start()

    def send_up(s):
        return pltpu.make_async_remote_copy(
            src_ref=own.at[s], dst_ref=came.at[s], send_sem=up_send.at[s], recv_sem=in_recv.at[s],
            device_id={"dp": up}, device_id_type=MESH,
        )

    def swap(s):
        return pltpu.make_async_remote_copy(
            src_ref=own.at[s], dst_ref=tot.at[s], send_sem=up_send.at[s], recv_sem=tot_recv.at[s],
            device_id={"dp": up}, device_id_type=MESH,
        )

    def send_total(s):
        return pltpu.make_async_remote_copy(
            src_ref=tot.at[s], dst_ref=tot.at[s], send_sem=tot_send.at[s], recv_sem=tot_recv.at[s],
            device_id={"dp": out}, device_id_type=MESH,
        )

    def partial_on(s):
        @pl.when(relay)
        def _():
            send_up(s).wait_recv()
            own[s] = own[s] + came[s]

        @pl.when(center)
        def _():
            swap(s).start()

        @pl.when(edge)
        def _():
            send_up(s).start()

    def total_on(s, target, c):
        swap(s).wait_recv()

        @pl.when(center)
        def _():
            tot[s] = tot[s] + own[s]

        @pl.when(relay)
        def _():
            send_total(s).start()

        pltpu.make_async_copy(tot.at[s], target.at[:, columns(c)], sum_out.at[s]).start()

    def totals(s):
        @pl.when(s < count)
        def _():
            total_on(s, bias_out, s)

        @pl.when(s >= count)
        def _():
            total_on(s, gain_out, s - count)

    lag = jnp.where(center, 2, 8)

    def slot(s):
        partial_on(s)

        @pl.when(s >= lag)
        def _():
            totals(s - lag)

    slots = [order[0, j] for j in range(MB)]
    place = []
    for m in range(MB):
        found = 0
        for j in range(MB):
            found = jnp.where(slots[j] == m, j, found)
        place.append(found)

    load_cot.wait()

    def bias_part(c):
        cols = columns(c)
        for m in range(MB):
            cot_fwd[c, m * per : (m + 1) * per, :] = cot_raw[place[m], :, cols]
        own[c] = jnp.dot(sel_t2[:, :tokens], cot_fwd[c], preferred_element_type=F32)

    for t in range(n_tensor):
        pltpu.make_async_remote_copy(
            src_ref=mom_own, dst_ref=mom_in.at[t], send_sem=mom_send.at[t], recv_sem=mom_recv.at[t],
            device_id={"pipe": after}, device_id_type=MESH,
        ).wait_recv()
    moment = mom_in[0]
    for t in range(1, n_tensor):
        moment = moment + mom_in[t]
    mean = moment[:, 0:1] / D
    spread = moment[:, 1:2] / D - mean * mean
    rows[0] = jnp.broadcast_to(mean, (tokens, LANES))
    rows[1] = jnp.broadcast_to(lax.rsqrt(spread + EPS), (tokens, LANES))
    cross_in[tensor] = zeros
    rows[2] = zeros
    rows[3] = zeros

    def wide(value):
        return jnp.concatenate([value] * (CW // LANES), axis=1)

    @pl.loop(0, count)
    def _(c):
        cols = columns(c)

        bias_part(c)
        slot(c)

        @pl.when(first)
        def _():
            load_x(c).wait()

        @pl.when(jnp.logical_not(first))
        def _():
            send_x(c).wait_recv()

        @pl.when(jnp.logical_not(last))
        def _():
            send_x(c).wait_send()

            @pl.when(c + AHEAD < count)
            def _():
                send_x(c + AHEAD).start()

        gain_rows = jnp.dot(sel[...], gain[:, cols], preferred_element_type=F32)
        bias_rows = jnp.dot(sel[...], bias[:, cols], preferred_element_type=F32)
        xn = (x_buf[c].astype(F32) - wide(rows[0])) * wide(rows[1])
        n_buf[c] = (xn * gain_rows + bias_rows).astype(BF16)
        pltpu.make_async_copy(n_buf.at[c], normed_out.at[:, cols], n_out.at[c]).start()
        ct = cot_fwd[c].astype(F32)
        sc = ct * gain_rows
        rows[2] = rows[2] + fold(sc)
        rows[3] = rows[3] + fold(sc * xn)
        xn_buf[c] = xn
        sc_buf[c] = sc
        product = ct * xn
        high = product.astype(BF16)
        low = (product - high.astype(F32)).astype(BF16)
        own[count + c] = jnp.dot(
            sel_t2[...], jnp.concatenate([high, low], axis=0), preferred_element_type=F32
        )

    cross_own[...] = pack(rows[2], rows[3])

    def send_cross(t):
        return pltpu.make_async_remote_copy(
            src_ref=cross_own, dst_ref=cross_in.at[tensor],
            send_sem=cross_send.at[t], recv_sem=cross_recv.at[tensor],
            device_id={"tensor": lax.rem(tensor + t, n_tensor)}, device_id_type=MESH,
        )

    for t in range(1, n_tensor):
        send_cross(t).start()
    slot(count)
    for t in range(1, n_tensor):
        other = lax.rem(tensor + t, n_tensor)
        pltpu.make_async_remote_copy(
            src_ref=cross_own, dst_ref=cross_in.at[other],
            send_sem=cross_send.at[t], recv_sem=cross_recv.at[other],
            device_id={"tensor": other}, device_id_type=MESH,
        ).wait_recv()
    cross = cross_own[...]
    for t in range(n_tensor):
        cross = cross + cross_in[t]
    rows[2] = jnp.broadcast_to(cross[:, 0:1] / D, (tokens, LANES))
    rows[3] = jnp.broadcast_to(cross[:, 1:2] / D, (tokens, LANES))
    load_res.wait()

    def send_grad(c):
        return pltpu.make_async_remote_copy(
            src_ref=g_buf.at[c], dst_ref=grad_out.at[:, columns(c)],
            send_sem=g_send.at[c], recv_sem=g_recv.at[c],
            device_id={"pipe": before}, device_id_type=MESH,
        )

    def grad_part(c):
        cols = columns(c)
        for m in range(MB):
            span = slice(m * per, (m + 1) * per)
            inner = sc_buf[c, span, :] - wide(rows[2, span, :]) - xn_buf[c, span, :] * wide(rows[3, span, :])
            g_tmp[m] = (
                res_raw[place[m], :, cols].astype(F32) + wide(rows[1, span, :]) * inner
            ).astype(BF16)
        for j in range(MB):
            g_buf[c, j * per : (j + 1) * per, :] = g_tmp[slots[j]]
        send_grad(c).start()

    both = count // 2

    @pl.loop(0, both)
    def _(i):
        grad_part(2 * i)
        grad_part(2 * i + 1)

        slot(count + 1 + i)

    @pl.loop(count + 1 + both, 2 * count)
    def _(s):
        slot(s)

    @pl.loop(jnp.maximum(2 * count - lag, 0), 2 * count)
    def _(s):
        totals(s)

    for t in range(n_tensor):
        send_moments(t).wait_send()
    for t in range(1, n_tensor):
        send_cross(t).wait_send()

    @pl.loop(0, count)
    def _(c):
        pltpu.make_async_copy(n_buf.at[c], normed_out.at[:, columns(c)], n_out.at[c]).wait()
        send_grad(c).wait_send()
        send_grad(c).wait_recv()

    @pl.loop(0, 2 * count)
    def _(s):
        send_up(s).wait_send()

        @pl.when(relay)
        def _():
            send_total(s).wait_send()

        pltpu.make_async_copy(tot.at[s], bias_out.at[:, pl.ds(0, CW)], sum_out.at[s]).wait()


def local(section_out, embedded, cot_norm, cot_res, gain, bias, lang_ids, mb_order):
    n_dp, n_pipe, n_tensor = (lax.axis_size(axis) for axis in ("dp", "pipe", "tensor"))
    tokens, width = embedded.shape
    langs = gain.shape[1]
    per = tokens // MB
    count = width // CW
    dma = pltpu.SemaphoreType.DMA
    normed, grad, gain_grad, bias_grad = pl.pallas_call(
        functools.partial(kernel, n_dp, n_pipe, n_tensor),
        out_shape=(
            jax.ShapeDtypeStruct((tokens, width), BF16),
            jax.ShapeDtypeStruct((tokens, width), BF16),
            jax.ShapeDtypeStruct((langs, width), F32),
            jax.ShapeDtypeStruct((langs, width), F32),
        ),
        in_specs=[ANY, ANY, ANY, ANY, VMEM, VMEM, VMEM, SMEM],
        out_specs=(ANY, ANY, ANY, ANY),
        scratch_shapes=[
            pltpu.VMEM((tokens, width), BF16),
            pltpu.VMEM((MB, per, width), BF16),
            pltpu.VMEM((MB, per, width), BF16),
            pltpu.VMEM((count, tokens, CW), BF16),
            pltpu.VMEM((count, tokens, CW), BF16),
            pltpu.VMEM((count, tokens, CW), F32),
            pltpu.VMEM((count, tokens, CW), F32),
            pltpu.VMEM((count, tokens, CW), BF16),
            pltpu.VMEM((count, tokens, CW), BF16),
            pltpu.VMEM((MB, per, CW), BF16),
            pltpu.VMEM((2 * count, langs, CW), F32),
            pltpu.VMEM((2 * count, langs, CW), F32),
            pltpu.VMEM((2 * count, langs, CW), F32),
            pltpu.VMEM((tokens, LANES), F32),
            pltpu.VMEM((n_tensor, tokens, LANES), F32),
            pltpu.VMEM((tokens, LANES), F32),
            pltpu.VMEM((n_tensor, tokens, LANES), F32),
            pltpu.VMEM((4, tokens, LANES), F32),
            pltpu.VMEM((langs, 2 * tokens), BF16),
            pltpu.VMEM((tokens, langs), BF16),
            dma((3,)), dma((count,)), dma((count,)),
            dma((n_tensor,)), dma((n_tensor,)), dma((n_tensor,)), dma((n_tensor,)),
            dma((2 * count,)), dma((2 * count,)), dma((2 * count,)), dma((2 * count,)),
            dma((2 * count,)), dma((count,)), dma((count,)), dma((count,)),
        ],
        compiler_params=pltpu.CompilerParams(
            collective_id=0, has_side_effects=True, vmem_limit_bytes=56 * 1024 * 1024
        ),
        cost_estimate=pl.CostEstimate(flops=10**9, bytes_accessed=16 * 2**20, transcendentals=0),
    )(
        section_out, embedded,
        cot_norm.reshape(MB, per, width), cot_res.reshape(MB, per, width),
        gain[0], bias[0], lang_ids.reshape(1, tokens), mb_order,
    )
    return normed[None], grad[None], gain_grad[None], bias_grad[None]


def solution(mesh):
    return jax.shard_map(
        local,
        mesh=mesh,
        in_specs=(
            P("pipe", "dp", "tensor"),
            P("dp", "tensor"),
            P("pipe", "dp", "tensor"),
            P("pipe", "dp", "tensor"),
            P("pipe", None, "tensor"),
            P("pipe", None, "tensor"),
            P("dp"),
            P("dp", None),
        ),
        out_specs=(
            P("pipe", "dp", "tensor"),
            P("pipe", "dp", "tensor"),
            P("pipe", None, "tensor"),
            P("pipe", None, "tensor"),
        ),
        check_vma=False,
    )
```

time: 198 us -> 101 us (0.51)
  waiting for transfers between devices: 125 us -> 0 us
  Pallas kernels: 0 us -> 92.7 us
  other arithmetic: 18.3 us -> 0 us
  between operations: 14.1 us -> 0.65 us
  matrix products: 12.1 us -> 0 us
  starting transfers between devices: 9.77 us -> 0 us
  local copies, waits for them, and re-layouts: 13.5 us -> 7.9 us
  blocking collectives: 4.91 us -> 0 us
    pallas_call x0 -> x1, Pallas kernels: none -> 92.7 us  [local(): pl.pallas_call(functools.partial(kernel, n_dp, n_pipe, n_tensor), out_sha...]
    psum x1 -> x0, waiting for transfers between devices: 72.8 us -> none  [local(): summed = lax.psum(local_sums, 'dp')]
    ppermute x2 -> x0, waiting for transfers between devices: 52.5 us -> none  [the longest x1 30.8 us: passed_along(): lax.ppermute(array, axis, [(i, (i + by) % length) for i in range(length)])]
    dot_general x3 -> x0, matrix products: 12.1 us -> none  [the longest x1 4.63 us: local(): gain_rows = jnp.dot(selector, gain[0], preferred_element_type=jnp.float32)]
    ppermute x2 -> x0, starting transfers between devices: 9.73 us -> none  [the longest x1 6.27 us: shifted(): lax.ppermute(value, axis, [(source, source + steps) for source in range(l...]
    convert_element_type x2 -> x0, other arithmetic: 7.7 us -> none  [the longest x1 5.57 us: local(): (pass_fwd + inv_scale * (scaled_cot - mean_cot - normalized * mean_cross)...]
    gather x3 -> x0, local copies, waits for them, and re-layouts: 6.92 us -> none  [reorder(): return jnp.take(shaped, order, axis=0).reshape(values.shape)]
    select_n x4 -> x0, other arithmetic: 5.8 us -> none  [reorder(): return jnp.take(shaped, order, axis=0).reshape(values.shape)]
  transfers between devices with their start and end apart: 3 -> 0, of which waited for: 3 -> 0; matrix products, arithmetic and copies ran while one was open for 13% -> 0% of each run, Pallas kernels for 0% -> 0%
where the time goes in v1:
time: 101 us
  Pallas kernels  92.7 us (92%)
  local copies, waits for them, and re-layouts  7.9 us (8%)
    pallas_call x1, Pallas kernels, local(): pl.pallas_call(functools.partial(kernel, n_dp, n_pipe, n_tensor), out_sha...  92.7 us
    unnamed x10, local copies, waits for them, and re-layouts  7.9 us

profile of v1, /device:TPU:0, one launch (start us, length us, event | category | flops | bytes accessed | tf_op | source)
XLA Modules:
  0.0 101.3 jit_solution(13202680267369865055)
XLA Ops:
  0.6 92.7 %shard_map.111 = (bf16[128,6144]{1,0:T(8,128)(2,1)}, bf16[128,6144]{1,0:T(8,128)(2,1)}, f32[64,6144]{1,0:T(8,128)}, f32[64,6144]{1,0:T(8,128)}) custom-call(bf16[1,128,6144]{2,1,0:T(8,128)(2,1)} %section.1, bf16[128,6144]{1,0:T(8,128)(2,1)} %embedded.1, bf16[4,32,6144]{2,1,0:T(8,128)(2,1)} %bitcast.13, bf16[4,32,6144]{2,1,0:T(8,128)(2,1)} %bitcast.14, ...), custom_call_target="tpu_custom_call" | custom-call | flops 1000000000 | bytes 16777216 | tf_op jit(solution)/shard_map/pallas_call | solution.py:370
  93.3 0.0 copy-start.2
  93.4 2.8 %copy.16 = bf16[1,128,6144]{2,1,0:T(8,128)(2,1)} copy(bf16[1,128,6144]{2,1,0:T(8,128)(2,1)} %bitcast.12) | data formatting | bytes 3145728
  96.2 0.0 copy-done.2
  96.2 0.0 copy-start.1
  96.2 1.1 %copy.17 = bf16[1,128,6144]{2,1,0:T(8,128)(2,1)} copy(bf16[1,128,6144]{2,1,0:T(8,128)(2,1)S(1)} %bitcast.11) | data formatting | bytes 3145728
  97.3 0.8 copy-done.1
  98.1 0.0 copy-start
  98.1 1.1 %copy.18 = f32[1,64,6144]{2,1,0:T(8,128)} copy(f32[1,64,6144]{2,1,0:T(8,128)S(1)} %bitcast.10) | data formatting | bytes 3145728
  99.3 0.8 copy-done
  100.1 1.1 %copy.19 = f32[1,64,6144]{2,1,0:T(8,128)} copy(f32[1,64,6144]{2,1,0:T(8,128)S(1)} %bitcast.9) | data formatting | bytes 3145728
Async XLA Ops:
  93.3 2.8 %copy-start.2 = (bf16[128,6144]{1,0:T(8,128)(2,1)S(1)}, bf16[128,6144]{1,0:T(8,128)(2,1)}, u32[]{:S(2)}) copy-start(bf16[128,6144]{1,0:T(8,128)(2,1)} %get-tuple-element.9) | copy-start | bytes 4718596
  96.2 2.0 %copy-start.1 = (f32[64,6144]{1,0:T(8,128)S(1)}, f32[64,6144]{1,0:T(8,128)}, u32[]{:S(2)}) copy-start(f32[64,6144]{1,0:T(8,128)} %get-tuple-element.10) | copy-start | bytes 4718596
  98.1 2.0 %copy-start = (f32[64,6144]{1,0:T(8,128)S(1)}, f32[64,6144]{1,0:T(8,128)}, u32[]{:S(2)}) copy-start(f32[64,6144]{1,0:T(8,128)} %get-tuple-element.11) | copy-start | bytes 4718596
